TPU v7x, 256 devices: a whole 4x4x8 slice. The times are simulated.
256 devices in a mesh: blk: 32 (over x, z), grp: 8 (over y, core).
Axes of the slice: x: 4, y: 4, z: 8, core: 2. Of those that a mesh axis runs over, the one named last changes fastest.
Arguments:
- features: bfloat16 [8, 8192, 256], P('grp', 'blk'), may hold values from -6 to 6
- weight: bfloat16 [256, 256], replicated, may hold values from -0.375 to 0.375
- cotangent: bfloat16 [8, 8192, 256], P('grp', 'blk'), may hold values from -6 to 6
- dense_tiles: bfloat16 [8, 32, 64, 128, 128], P('grp', 'blk'), as said below
- dense_cols: int32 [8, 32, 64], P('grp', 'blk'), may hold values from 0 to 1, as said below
- sparse_tiles: bfloat16 [8, 32, 32, 128, 128], P('grp', 'blk'), may hold values from -0.09375 to 0.09375
- sparse_rows: int32 [8, 32, 32], P('grp', 'blk'), may hold values from 0 to 1
- sparse_cols: int32 [8, 32, 32], P('grp', 'blk'), may hold values from 0 to 7
- send_rows: int32 [8, 32, 8, 128], P('grp', 'blk'), may hold values from 0 to 255
- send_counts: int32 [8, 32, 8], P('grp', 'blk'), may hold values from 16 to 128, as said below
Outputs:
- hidden: bfloat16 [8, 8192, 256], P('grp', 'blk')
- grad_features: bfloat16 [8, 8192, 256], P('grp', 'blk')
- grad_weight: float32 [256, 256], replicated
Inputs may be any that keep to these rules, and one draw needn't show every extreme that they name: Tile t of device (g, b) has row tile t % 2 and source block t // 2; for one device and one source block the 2 tiles name distinct column tiles, and the adjacency given by dense_tiles and dense_cols inside each group is symmetric. `dense_tiles`: together with dense_cols the tiles give a symmetric adjacency inside each group. `send_counts`: entry [s, b, g] counts the rows that device (s, b) sends to device (g, b); for every block index some receiver gets 128 rows from every sender.
All inputs are finite; a program needn't handle non-finite values.
Results may differ from a plain program's by a relative error of at most 0.0065.
Values may be sent and summed in bfloat16 or wider, within the bound.
No kernel may reach another device: no remote copies, remote signals or barrier semaphores. Data moves between devices by JAX's collectives and lax.ppermute only.
A program may use at most 64 MiB of HBM per device.

v0:
```python
import jax
import jax.numpy as jnp
from jax import lax
from jax.sharding import PartitionSpec as P


def body(
    features,
    weight,
    cotangent,
    dense_tiles,
    dense_cols,
    sparse_tiles,
    sparse_rows,
    sparse_cols,
    send_rows,
    send_counts,
):
    row_count = features.shape[1]
    hidden_width = weight.shape[1]
    tile_values = dense_tiles[0, 0]
    tile_cols = dense_cols[0, 0]
    tile_size = tile_values.shape[-1]
    row_tiles = row_count // tile_size
    projected = jnp.dot(features[0], weight, preferred_element_type=jnp.float32).astype(
        jnp.bfloat16
    )
    send_list = send_rows[0, 0]
    send_count = send_counts[0, 0]
    capacity = send_list.shape[1]
    in_use = jnp.arange(capacity)[None, :] < send_count[:, None]
    outgoing = jnp.where(in_use[:, :, None], projected[send_list], jnp.zeros((), jnp.bfloat16))
    received = lax.all_to_all(outgoing, "grp", split_axis=0, concat_axis=0, tiled=True)
    shards = lax.all_gather(projected, "blk", axis=0, tiled=True)
    block_count = shards.shape[0] // row_count
    chosen = tile_values
    chosen_cols = tile_cols
    positions = jnp.arange(block_count * row_tiles) // row_tiles * row_tiles + chosen_cols
    source = shards.reshape(block_count * row_tiles, tile_size, hidden_width)[positions]
    dense_part = jnp.einsum(
        "crij,crjh->rih",
        chosen.reshape(block_count, row_tiles, tile_size, tile_size),
        source.reshape(block_count, row_tiles, tile_size, hidden_width),
        preferred_element_type=jnp.float32,
    )
    sparse_vals = sparse_tiles[0, 0]
    row_slot = sparse_rows[0, 0]
    col_block = sparse_cols[0, 0]
    recv_count = received.shape[0]
    products = jnp.einsum(
        "uij,ujh->uih", sparse_vals, received[col_block], preferred_element_type=jnp.float32
    )
    row_pick = (row_slot[:, None] == jnp.arange(row_tiles)[None, :]).astype(jnp.float32)
    sparse_part = jnp.einsum("ur,uih->rih", row_pick, products, precision=lax.Precision.HIGHEST)
    pre_act = (dense_part + sparse_part).reshape(row_count, hidden_width)
    sigmoid_pre = jax.nn.sigmoid(pre_act)
    hidden = (pre_act * sigmoid_pre).astype(jnp.bfloat16)
    grad_pre = (
        cotangent[0].astype(jnp.float32) * sigmoid_pre * (1.0 + pre_act * (1.0 - sigmoid_pre))
    ).astype(jnp.bfloat16)
    grad_tiles = grad_pre.reshape(row_tiles, tile_size, hidden_width)
    block_count = row_count * lax.axis_size("blk") // row_count
    chosen = tile_values
    chosen_cols = tile_cols
    chosen = chosen.reshape(block_count, row_tiles, tile_size, tile_size)
    chosen_cols = chosen_cols.reshape(block_count, row_tiles)
    moved = jnp.einsum("crij,rih->crjh", chosen, grad_tiles, preferred_element_type=jnp.float32)
    pieces = [
        jnp.sum(jnp.where((chosen_cols == target)[:, :, None, None], moved, 0.0), axis=1)
        for target in range(row_tiles)
    ]
    dense_back = lax.psum_scatter(
        jnp.stack(pieces, axis=1).reshape(row_count * lax.axis_size("blk"), hidden_width),
        "blk",
        scatter_dimension=0,
        tiled=True,
    )
    tile_grads = jnp.einsum(
        "uij,uih->ujh", sparse_vals, grad_tiles[row_slot], preferred_element_type=jnp.float32
    )
    block_pick = (col_block[:, None] == jnp.arange(recv_count)[None, :]).astype(jnp.float32)
    slot_grad = jnp.einsum("uq,ujh->qjh", block_pick, tile_grads, precision=lax.Precision.HIGHEST)
    returned = lax.all_to_all(slot_grad, "grp", split_axis=0, concat_axis=0, tiled=True)
    returned = jnp.where(in_use[:, :, None], returned, 0.0)
    sparse_back = (
        jnp.zeros((row_count, hidden_width), jnp.float32)
        .at[send_list.reshape(-1)]
        .add(returned.reshape(-1, hidden_width))
    )
    agg_grad = (dense_back + sparse_back).astype(jnp.bfloat16)
    grad_features = jnp.einsum(
        "rh,fh->rf", agg_grad, weight, preferred_element_type=jnp.float32
    ).astype(jnp.bfloat16)
    partial_weight = jnp.einsum(
        "rf,rh->fh", features[0], agg_grad, preferred_element_type=jnp.float32
    )
    vertex_total = row_count * lax.axis_size("blk") * lax.axis_size("grp")
    grad_weight = lax.psum(partial_weight, ("blk", "grp")) * float(vertex_total) ** (-0.5)
    return (hidden[None], grad_features[None], grad_weight)


def solution(mesh):
    placed = (
        P("grp", "blk", None),
        P(),
        P("grp", "blk", None),
        P("grp", "blk", None, None, None),
        P("grp", "blk", None),
        P("grp", "blk", None, None, None),
        P("grp", "blk", None),
        P("grp", "blk", None),
        P("grp", "blk", None, None),
        P("grp", "blk", None),
    )
    return jax.shard_map(
        body,
        mesh=mesh,
        in_specs=placed,
        out_specs=(P("grp", "blk", None), P("grp", "blk", None), P()),
        check_vma=False,
    )
```

profile of v0, /device:TPU:2, one launch (start us, length us, event | category | flops | bytes accessed | tf_op | source)
XLA Modules:
  0.0 613.4 jit_solution(7899231333244268528)
XLA Ops:
  7.3 1.9 convolution_convert_fusion.1
  9.9 4.4 gather_fusion.1
  15.4 4.5 all-to-all-start
  20.5 9.8 %all-to-all-done = bf16[8,128,256]{2,1,0:T(8,128)(2,1)S(1)} async-done(((bf16[8,128,256]{2,1,0:T(8,128)(2,1)}), bf16[8,128,256]{2,1,0:T(8,128)(2,1)S(1)}, u32[]{:S(2)}, u32[]{:S(2)}) %all-to-all-start) | async-done | bytes 524320 | tf_op jit(solution)/shard_map/all_to_all | solution.py:33
  30.2 2.0 gather_fusion.2
  32.3 4.6 convolution_bitcast_fusion.1
  36.9 5.5 copy.32
  42.4 3.6 fusion.25
  46.0 48.7 %all-gather.2.cloned.1.call-done = bf16[8192,256]{1,0:T(8,128)(2,1)} async-done(((bf16[256,256]{1,0:T(8,128)(2,1)}), bf16[8192,256]{1,0:T(8,128)(2,1)}) %all-gather.2.cloned.1.call-update) | async-done | bytes 4194320 | tf_op jit(solution)/shard_map/all_gather | solution.py:34
  94.7 5.0 gather_fusion
  99.7 3.0 fusion.9
  102.7 3.4 fusion
  106.0 3.8 pad_maximum_fusion
  109.8 9.0 %copy.38 = f32[32,2,128,256]{3,2,1,0:T(8,128)} copy(f32[32,2,128,256]{2,3,0,1:T(8,128)} %pad_maximum_fusion) | data formatting | bytes 16777216 | tf_op jit(solution)/shard_map/stack | solution.py:73
  118.8 2.0 gather_fusion.3
  120.9 4.3 convolution_bitcast_fusion
  125.1 5.5 copy.40
  130.6 3.7 fusion.22
  135.6 4.3 all-to-all-start.1
  140.1 15.8 %all-to-all-done.1 = f32[8,128,256]{2,1,0:T(8,128)} async-done(((f32[8,128,256]{2,1,0:T(8,128)}), f32[8,128,256]{2,1,0:T(8,128)}, u32[]{:S(2)}, u32[]{:S(2)}) %all-to-all-start.1) | async-done | bytes 1048608 | tf_op jit(solution)/shard_map/all_to_all | solution.py:83
  157.4 188.5 %reduce-scatter.2.cloned.1.call-done = f32[256,256]{1,0:T(8,128)} async-done(((f32[8192,256]{1,0:T(8,128)}), f32[256,256]{1,0:T(8,128)}) %reduce-scatter.2.cloned.1.call-update) | async-done | bytes 262160 | tf_op jit(solution)/shard_map/reduce_scatter | solution.py:72
  345.9 7.7 %scatter_fusion = f32[256,256]{1,0:T(8,128)} fusion(f32[256,256]{1,0:T(8,128)} %reduce-scatter.2.cloned.1.call-done, s32[1024]{0:T(1024)S(1)} %bitcast.110, f32[1024,256]{1,0:T(8,128)S(1)} %bitcast.103), kind=kCustom, calls=%fused_computation.4 | custom fusion | flops 262144 | bytes 3149824 | tf_op jit(solution)/shard_map/scatter-add | solution.py:88
  353.5 1.9 convolution_bitcast_fusion.3
  358.0 247.0 %all-reduce.2.cloned.1.call-done = f32[256,256]{0,1:T(8,128)} async-done(((f32[256,256]{0,1:T(8,128)}), f32[256,256]{0,1:T(8,128)}) %all-reduce.2.cloned.1.call-update) | async-done | bytes 262160 | tf_op jit(solution)/shard_map/psum | solution.py:98
  (45 shorter events, 9.8 us)
Async XLA Ops:
  7.2 92.5 %copy-start = (bf16[1,1,64,128,128]{4,3,2,1,0:T(8,128)(2,1)S(1)}, bf16[1,1,64,128,128]{4,3,2,1,0:T(8,128)(2,1)}, u32[]{:S(2)}) copy-start(bf16[1,1,64,128,128]{4,3,2,1,0:T(8,128)(2,1)} %param.13) | copy-start | bytes 6291460
  7.2 7.1 %copy-start.7 = (s32[1,1,8]{2,1,0:T(1,128)S(1)}, s32[1,1,8]{2,1,0:T(1,128)}, u32[]{:S(2)}) copy-start(s32[1,1,8]{2,1,0:T(1,128)} %param.19) | copy-start | bytes 100
  7.2 12.7 %copy-start.6 = (s32[1,1,32]{2,1,0:T(1,128)S(1)}, s32[1,1,32]{2,1,0:T(1,128)}, u32[]{:S(2)}) copy-start(s32[1,1,32]{2,1,0:T(1,128)} %param.17) | copy-start | bytes 388
  7.2 12.8 %copy-start.8 = (s32[1,1,64]{2,1,0:T(1,128)S(1)}, s32[1,1,64]{2,1,0:T(1,128)}, u32[]{:S(2)}) copy-start(s32[1,1,64]{2,1,0:T(1,128)} %param.14) | copy-start | bytes 772
  7.2 87.5 %all-gather.2.cloned.1.call-start = ((), (), s32[]{:S(2)}) async-start(), calls=%async_computation.3 | async-start | bytes 4325376 | tf_op jit(solution)/shard_map/all_gather | solution.py:34
  15.4 14.8 %all-to-all-start = ((bf16[8,128,256]{2,1,0:T(8,128)(2,1)}), bf16[8,128,256]{2,1,0:T(8,128)(2,1)S(1)}, u32[]{:S(2)}, u32[]{:S(2)}) async-start(bf16[8,128,256]{2,1,0:T(8,128)(2,1)} %broadcast_select_fusion.1), calls=%async_computation | async-start | bytes 1048576 | tf_op jit(solution)/shard_map/all_to_all | solution.py:33
  19.9 326.0 %reduce-scatter.2.cloned.1.call-start = ((), (), s32[]{:S(2)}) async-start(), calls=%async_computation.4 | async-start | bytes 8650752 | tf_op jit(solution)/shard_map/reduce_scatter | solution.py:72
  36.9 5.5 copy-start.5
  94.7 5.0 copy-start.3
  118.8 2.1 copy-start.1
  130.6 9.5 %copy-start.4 = (s32[1,1,8,128]{3,2,1,0:T(8,128)S(1)}, s32[1,1,8,128]{3,2,1,0:T(8,128)}, u32[]{:S(2)}) copy-start(s32[1,1,8,128]{3,2,1,0:T(8,128)} %param.18) | copy-start | bytes 12292
  135.6 20.4 %all-to-all-start.1 = ((f32[8,128,256]{2,1,0:T(8,128)}), f32[8,128,256]{2,1,0:T(8,128)}, u32[]{:S(2)}, u32[]{:S(2)}) async-start(f32[8,128,256]{2,1,0:T(8,128)} %copy.41), calls=%async_computation.2 | async-start | bytes 2097152 | tf_op jit(solution)/shard_map/all_to_all | solution.py:83
  139.9 465.2 %all-reduce.2.cloned.1.call-start = ((), (), s32[]{:S(2)}) async-start(), calls=%async_computation.5 | async-start | bytes 524288 | tf_op jit(solution)/shard_map/psum | solution.py:98
  345.9 7.7 %copy-start.2 = (bf16[1,256,256]{2,1,0:T(8,128)(2,1)S(1)}, bf16[1,256,256]{2,1,0:T(8,128)(2,1)}, u32[]{:S(2)}) copy-start(bf16[1,256,256]{2,1,0:T(8,128)(2,1)} %param.10) | copy-start | bytes 393220
Sparse Core Ops, SparseCore 0:
  11.2 83.4 all-gather.1
  118.9 226.8 reduce-scatter.1
  355.6 249.4 all-reduce.1
where the time goes:
time: 614 us; the launch traced here: 613 us
  waiting for transfers between devices  510 us (83%)
  local copies, waits for them, and re-layouts  36 us (6%)
  matrix products  28.2 us (5%)
  other arithmetic  16.4 us (3%)
  between operations  13.9 us (2%)
  starting transfers between devices  9.05 us (1%)
    psum x1, waiting for transfers between devices, body(): lax.psum(partial_weight, ('blk', 'grp')) * float(vertex_total) ** (-0.5)  247 us
    reduce_scatter x1, waiting for transfers between devices, body(): lax.psum_scatter(jnp.stack(pieces, axis=1).reshape(row_count * lax.axis_s...  188 us
    all_gather x1, waiting for transfers between devices, body(): shards = lax.all_gather(projected, 'blk', axis=0, tiled=True)  48.7 us
    all_to_all x1, waiting for transfers between devices, body(): lax.all_to_all(slot_grad, 'grp', split_axis=0, concat_axis=0, tiled=True)  15.8 us
  transfers between devices with their start and end apart: 5, of which 5 were waited for; matrix products, arithmetic and copies ran while one was open for 7% of the time, Pallas kernels for 0%

commit v1 on v0

--- a/solution.py
+++ b/solution.py
@@ -95,7 +95,7 @@
         "rf,rh->fh", features[0], agg_grad, preferred_element_type=jnp.float32
     )
     vertex_total = row_count * lax.axis_size("blk") * lax.axis_size("grp")
-    grad_weight = lax.psum(partial_weight, ("blk", "grp")) * float(vertex_total) ** (-0.5)
+    grad_weight = lax.psum(lax.psum(partial_weight, "blk"), "grp") * float(vertex_total) ** (-0.5)
     return (hidden[None], grad_features[None], grad_weight)
 
 

time: 614 us -> 572 us (0.932)
  waiting for transfers between devices: 510 us -> 468 us
    psum x1 -> x2, waiting for transfers between devices: 247 us -> 205 us  [the longest x1 142 us: body(): lax.psum(partial_weight, 'blk')]
  transfers between devices with their start and end apart: 5 -> 6, of which waited for: 5 -> 6; matrix products, arithmetic and copies ran while one was open for 7% -> 8% of each run, Pallas kernels for 0% -> 0%
where the time goes in v1:
time: 572 us; the launch traced here: 571 us
  waiting for transfers between devices  468 us (82%)
  local copies, waits for them, and re-layouts  36 us (6%)
  matrix products  28.2 us (5%)
  other arithmetic  16.4 us (3%)
  between operations  14 us (2%)
  starting transfers between devices  9.1 us (2%)
    reduce_scatter x1, waiting for transfers between devices, body(): lax.psum_scatter(jnp.stack(pieces, axis=1).reshape(row_count * lax.axis_s...  188 us
    psum x1, waiting for transfers between devices, body(): lax.psum(partial_weight, 'blk')  142 us
    psum x1, waiting for transfers between devices, body(): lax.psum(lax.psum(partial_weight, 'blk'), 'grp')  62.8 us
    all_gather x1, waiting for transfers between devices, body(): shards = lax.all_gather(projected, 'blk', axis=0, tiled=True)  48.7 us
    all_to_all x1, waiting for transfers between devices, body(): lax.all_to_all(slot_grad, 'grp', split_axis=0, concat_axis=0, tiled=True)  15.8 us
  transfers between devices with their start and end apart: 6, of which 6 were waited for; matrix products, arithmetic and copies ran while one was open for 8% of the time, Pallas kernels for 0%

profile of v1, /device:TPU:2, one launch (start us, length us, event | category | flops | bytes accessed | tf_op | source)
XLA Modules:
  0.0 571.4 jit_solution(566846662258012668)
XLA Ops:
  7.3 1.9 convolution_convert_fusion.1
  9.9 4.4 gather_fusion.1
  15.4 4.5 all-to-all-start
  20.5 9.8 %all-to-all-done = bf16[8,128,256]{2,1,0:T(8,128)(2,1)S(1)} async-done(((bf16[8,128,256]{2,1,0:T(8,128)(2,1)}), bf16[8,128,256]{2,1,0:T(8,128)(2,1)S(1)}, u32[]{:S(2)}, u32[]{:S(2)}) %all-to-all-start) | async-done | bytes 524320 | tf_op jit(solution)/shard_map/all_to_all | solution.py:33
  30.2 2.0 gather_fusion.2
  32.3 4.6 convolution_bitcast_fusion.1
  36.9 5.5 copy.32
  42.4 3.6 fusion.25
  46.0 48.7 %all-gather.2.cloned.1.call-done = bf16[8192,256]{1,0:T(8,128)(2,1)} async-done(((bf16[256,256]{1,0:T(8,128)(2,1)}), bf16[8192,256]{1,0:T(8,128)(2,1)}) %all-gather.2.cloned.1.call-update) | async-done | bytes 4194320 | tf_op jit(solution)/shard_map/all_gather | solution.py:34
  94.7 5.0 gather_fusion
  99.7 3.0 fusion.9
  102.7 3.4 fusion
  106.0 3.8 pad_maximum_fusion
  109.8 9.0 %copy.38 = f32[32,2,128,256]{3,2,1,0:T(8,128)} copy(f32[32,2,128,256]{2,3,0,1:T(8,128)} %pad_maximum_fusion) | data formatting | bytes 16777216 | tf_op jit(solution)/shard_map/stack | solution.py:73
  118.8 2.0 gather_fusion.3
  120.9 4.3 convolution_bitcast_fusion
  125.1 5.5 copy.40
  130.6 3.7 fusion.22
  135.6 4.3 all-to-all-start.1
  140.1 15.8 %all-to-all-done.1 = f32[8,128,256]{2,1,0:T(8,128)} async-done(((f32[8,128,256]{2,1,0:T(8,128)}), f32[8,128,256]{2,1,0:T(8,128)}, u32[]{:S(2)}, u32[]{:S(2)}) %all-to-all-start.1) | async-done | bytes 1048608 | tf_op jit(solution)/shard_map/all_to_all | solution.py:83
  157.4 188.5 %reduce-scatter.2.cloned.1.call-done = f32[256,256]{1,0:T(8,128)} async-done(((f32[8192,256]{1,0:T(8,128)}), f32[256,256]{1,0:T(8,128)}) %reduce-scatter.2.cloned.1.call-update) | async-done | bytes 262160 | tf_op jit(solution)/shard_map/reduce_scatter | solution.py:72
  345.9 7.7 %scatter_fusion = f32[256,256]{1,0:T(8,128)} fusion(f32[256,256]{1,0:T(8,128)} %reduce-scatter.2.cloned.1.call-done, s32[1024]{0:T(1024)S(1)} %bitcast.110, f32[1024,256]{1,0:T(8,128)S(1)} %bitcast.103), kind=kCustom, calls=%fused_computation.4 | custom fusion | flops 262144 | bytes 3149824 | tf_op jit(solution)/shard_map/scatter-add | solution.py:88
  355.5 142.1 %all-reduce.3.cloned.1.call-done = f32[256,256]{0,1:T(8,128)} async-done(((f32[256,256]{0,1:T(8,128)}), f32[256,256]{0,1:T(8,128)}) %all-reduce.3.cloned.1.call-update) | async-done | bytes 262160 | tf_op jit(solution)/shard_map/psum | solution.py:98
  500.2 62.8 %all-reduce.5.cloned.1.call-done = f32[256,256]{0,1:T(8,128)} async-done(((f32[256,256]{0,1:T(8,128)}), f32[256,256]{0,1:T(8,128)}) %all-reduce.5.cloned.1.call-update) | async-done | bytes 262160 | tf_op jit(solution)/shard_map/psum | solution.py:98
  (48 shorter events, 11.7 us)
Async XLA Ops:
  7.2 92.5 %copy-start = (bf16[1,1,64,128,128]{4,3,2,1,0:T(8,128)(2,1)S(1)}, bf16[1,1,64,128,128]{4,3,2,1,0:T(8,128)(2,1)}, u32[]{:S(2)}) copy-start(bf16[1,1,64,128,128]{4,3,2,1,0:T(8,128)(2,1)} %param.13) | copy-start | bytes 6291460
  7.2 7.1 %copy-start.7 = (s32[1,1,8]{2,1,0:T(1,128)S(1)}, s32[1,1,8]{2,1,0:T(1,128)}, u32[]{:S(2)}) copy-start(s32[1,1,8]{2,1,0:T(1,128)} %param.19) | copy-start | bytes 100
  7.2 12.7 %copy-start.6 = (s32[1,1,32]{2,1,0:T(1,128)S(1)}, s32[1,1,32]{2,1,0:T(1,128)}, u32[]{:S(2)}) copy-start(s32[1,1,32]{2,1,0:T(1,128)} %param.17) | copy-start | bytes 388
  7.2 12.8 %copy-start.8 = (s32[1,1,64]{2,1,0:T(1,128)S(1)}, s32[1,1,64]{2,1,0:T(1,128)}, u32[]{:S(2)}) copy-start(s32[1,1,64]{2,1,0:T(1,128)} %param.14) | copy-start | bytes 772
  7.2 87.5 %all-gather.2.cloned.1.call-start = ((), (), s32[]{:S(2)}) async-start(), calls=%async_computation.3 | async-start | bytes 4325376 | tf_op jit(solution)/shard_map/all_gather | solution.py:34
  15.4 14.8 %all-to-all-start = ((bf16[8,128,256]{2,1,0:T(8,128)(2,1)}), bf16[8,128,256]{2,1,0:T(8,128)(2,1)S(1)}, u32[]{:S(2)}, u32[]{:S(2)}) async-start(bf16[8,128,256]{2,1,0:T(8,128)(2,1)} %broadcast_select_fusion.1), calls=%async_computation | async-start | bytes 1048576 | tf_op jit(solution)/shard_map/all_to_all | solution.py:33
  19.9 326.0 %reduce-scatter.2.cloned.1.call-start = ((), (), s32[]{:S(2)}) async-start(), calls=%async_computation.4 | async-start | bytes 8650752 | tf_op jit(solution)/shard_map/reduce_scatter | solution.py:72
  36.9 5.5 copy-start.5
  94.7 5.0 copy-start.3
  118.8 2.1 copy-start.1
  130.6 9.5 %copy-start.4 = (s32[1,1,8,128]{3,2,1,0:T(8,128)S(1)}, s32[1,1,8,128]{3,2,1,0:T(8,128)}, u32[]{:S(2)}) copy-start(s32[1,1,8,128]{3,2,1,0:T(8,128)} %param.18) | copy-start | bytes 12292
  135.6 20.4 %all-to-all-start.1 = ((f32[8,128,256]{2,1,0:T(8,128)}), f32[8,128,256]{2,1,0:T(8,128)}, u32[]{:S(2)}, u32[]{:S(2)}) async-start(f32[8,128,256]{2,1,0:T(8,128)} %copy.41), calls=%async_computation.2 | async-start | bytes 2097152 | tf_op jit(solution)/shard_map/all_to_all | solution.py:83
  139.9 357.7 %all-reduce.3.cloned.1.call-start = ((), (), s32[]{:S(2)}) async-start(), calls=%async_computation.5 | async-start | bytes 524288 | tf_op jit(solution)/shard_map/psum | solution.py:98
  345.9 7.7 %copy-start.2 = (bf16[1,256,256]{2,1,0:T(8,128)(2,1)S(1)}, bf16[1,256,256]{2,1,0:T(8,128)(2,1)}, u32[]{:S(2)}) copy-start(bf16[1,256,256]{2,1,0:T(8,128)(2,1)} %param.10) | copy-start | bytes 393220
  355.4 207.6 %all-reduce.5.cloned.1.call-start = ((), (), s32[]{:S(2)}) async-start(), calls=%async_computation.6 | async-start | bytes 524288 | tf_op jit(solution)/shard_map/psum | solution.py:98
Sparse Core Ops, SparseCore 0:
  11.2 83.4 all-gather.1
  118.9 226.8 reduce-scatter.1
  355.6 141.9 all-reduce.2
  499.9 63.0 all-reduce.4
